TPU v7x, 32 devices: a whole 2x2x4 slice. The times are simulated.
32 devices in a mesh: groups: 2 (over x), blk: 16 (over z, y, core).
Axes of the slice: x: 2, y: 2, z: 4, core: 2. Of those that a mesh axis runs over, the one named last changes fastest.
Arguments:
- density: bfloat16 [256, 9, 128, 128], P(('groups', 'blk')), parts along dimension 0, may hold values from -0.25 to 0.25
- ao_values: bfloat16 [384, 4, 128, 256], P(('groups', 'blk')), parts along dimension 0, may hold values from -6 to 6
- kernel: bfloat16 [384, 256, 256], P(('groups', 'blk')), parts along dimension 0, may hold values from -0.375 to 0.375
- grid_weights: float32 [384, 256], P(('groups', 'blk')), parts along dimension 0, may hold values from 0.002 to 0.02
- centre: int32 [384], P(('groups', 'blk')), parts along dimension 0, may hold values from 2 to 125, as said below
- sig_offsets: int32 [384, 4], P(('groups', 'blk')), parts along dimension 0, may hold values from -2 to 2, as said below
- counts: int32 [384], P(('groups', 'blk')), parts along dimension 0, may hold values from 0 to 4, as said below
Outputs:
- exchange: float32 [256, 9, 128, 128], P(('groups', 'blk')), parts along dimension 0
There are 2 independent parts, one for each index of `groups`. A program takes and returns all parts, laid end to end along the dimension named above; each array names one. Nothing has to cross between parts.
Inputs may be any that keep to these rules, and one draw needn't show every extreme that they name: `centre`: the batches in the rows of one blk device have their atom block among that device's 8 blocks; the device's first batch slot has the lowest such block that the range allows, its slot 10 the highest. `sig_offsets`: the 4 offsets of a batch are distinct; those of a device's first slot and of its slot 10 include -2 and 2. `counts`: the first batch slot and slot 10 of each blk device have 4 live blocks and its last slot none.
All inputs are finite; a program needn't handle non-finite values.
Results may differ from a plain program's by a relative error of at most 0.0041.
Values may be sent and summed in bfloat16 or wider, within the bound.
No kernel may reach another device: no remote copies, remote signals or barrier semaphores. Data moves between devices by JAX's collectives and lax.ppermute only.
A program may use at most 128 MiB of HBM per device.

v0:
```python
import jax
import jax.numpy as jnp
from jax import lax
from jax.sharding import PartitionSpec as P


def with_halo(shard, sides, width):
    for axis, dim in sides:
        size, length = (lax.axis_size(axis), shard.shape[dim])
        up = [(i, (i + 1) % size) for i in range(size - 1)]
        down = [(j, i) for i, j in up]
        last = lax.slice_in_dim(shard, length - width, length, axis=dim)
        initial = lax.slice_in_dim(shard, 0, width, axis=dim)
        before = lax.ppermute(last, axis, up)
        after = lax.ppermute(initial, axis, down)
        shard = jnp.concatenate([before, shard, after], axis=dim)
    return shard


def passed_along(shard, axis, by):
    length = lax.axis_size(axis)
    pairs = [(i, i + by) for i in range(length) if 0 <= i + by < length]
    return lax.ppermute(shard, axis, pairs)


def local(density, ao_values, kernel, grid_weights, centre, sig_offsets, counts):
    rows = density.shape[0]
    band_count = density.shape[1]
    half = (band_count - 1) // 2
    reach = half // 2
    slot_count = sig_offsets.shape[1]
    first = lax.axis_index("blk") * rows
    extended = with_halo(density, (("blk", 0),), reach)
    blocks = centre[:, None] + sig_offsets
    local_rows = blocks - first + reach
    live = jnp.arange(slot_count, dtype=jnp.int32)[None, :] < counts[:, None]
    panel = ao_values * live[:, :, None, None].astype(ao_values.dtype)
    bands = blocks[:, None, :] - blocks[:, :, None] + half
    tiles = extended[local_rows[:, :, None], bands]
    fpanel = jnp.einsum(
        "bkjxy,bjyg->bkxg", tiles, panel, preferred_element_type=jnp.float32
    ).astype(jnp.bfloat16)
    gpanel = jnp.einsum("bkxg,bgh->bkxh", fpanel, kernel, preferred_element_type=jnp.float32)
    hpanel = (
        gpanel * grid_weights[:, None, None, :] * live[:, :, None, None].astype(jnp.float32)
    ).astype(jnp.bfloat16)
    part = jnp.einsum("bkxg,bjyg->bkjxy", panel, hpanel, preferred_element_type=jnp.float32)
    accumulated = jnp.zeros((rows + 2 * reach,) + density.shape[1:], jnp.float32)
    accumulated = accumulated.at[local_rows[:, :, None], bands].add(part)
    own_rows = accumulated[reach : reach + rows]
    cut_low = 0
    lower_out = accumulated[:reach, cut_low:]
    upper_out = accumulated[rows + reach :, :band_count]
    from_left = passed_along(upper_out, "blk", 1)
    from_right = passed_along(lower_out, "blk", -1)
    own_rows = own_rows.at[:reach].add(from_left)
    own_rows = own_rows.at[rows - reach :].add(from_right)
    return own_rows


def solution(mesh):
    placed = (
        P(("groups", "blk"), None, None, None),
        P(("groups", "blk"), None, None, None),
        P(("groups", "blk"), None, None),
        P(("groups", "blk"), None),
        P(("groups", "blk")),
        P(("groups", "blk"), None),
        P(("groups", "blk")),
    )
    return jax.shard_map(
        local,
        mesh=mesh,
        in_specs=placed,
        out_specs=P(("groups", "blk"), None, None, None),
        check_vma=False,
    )
```

profile of v0, /device:TPU:1, one launch (start us, length us, event | category | flops | bytes accessed | tf_op | source)
XLA Modules:
  0.0 147.4 jit_solution(13013706999090434240)
XLA Ops:
  0.0 0.0 copy-start
  0.0 2.3 %fusion.22 = (bf16[2,9,128,128]{3,2,1,0:T(8,128)(2,1)}, bf16[2,9,128,128]{3,2,1,0:T(8,128)(2,1)S(1)}) fusion(bf16[8,9,128,128]{3,2,1,0:T(8,128)(2,1)} %param.11), kind=kLoop, calls=%fused_computation.38 | loop fusion | bytes 2359296 | tf_op jit(solution)/shard_map/slice | solution.py:12
  2.3 4.5 %collective-permute-start = (bf16[2,9,128,128]{3,2,1,0:T(8,128)(2,1)}, bf16[2,9,128,128]{3,2,1,0:T(8,128)(2,1)S(1)}, u32[]{:S(2)}, u32[]{:S(2)}) collective-permute-start(bf16[2,9,128,128]{3,2,1,0:T(8,128)(2,1)} %get-tuple-element.33), channel_id=1, source_target_pairs={{0,1},{1,2},{2,3},{3,4},{4,5},{5,6},{6,7},{7,8},{8,9},{9,10},{10,1... | collective-permute-start | bytes 1769480 | tf_op jit(solution)/shard_map/ppermute | solution.py:14
  6.8 1.9 %collective-permute-start.1 = (bf16[2,9,128,128]{3,2,1,0:T(8,128)(2,1)S(1)}, bf16[2,9,128,128]{3,2,1,0:T(8,128)(2,1)S(1)}, u32[]{:S(2)}, u32[]{:S(2)}) collective-permute-start(bf16[2,9,128,128]{3,2,1,0:T(8,128)(2,1)S(1)} %get-tuple-element.34), channel_id=1, source_target_pairs={{1,0},{2,1},{3,2},{4,3},{5,4},{6,5},{7,6},{8,7},{9,8},{10,9},{11,1... | collective-permute-start | bytes 1769480 | tf_op jit(solution)/shard_map/ppermute | solution.py:15
  8.7 0.7 clamp_shift-left_fusion.1
  9.4 0.1 copy.13
  9.5 0.1 copy.12
  9.7 0.1 copy.15
  9.7 0.1 fusion.16
  9.9 0.1 reshape.136
  10.0 0.1 reshape.142
  10.1 0.7 fusion.20
  10.8 9.4 %collective-permute-done = bf16[2,9,128,128]{3,2,1,0:T(8,128)(2,1)S(1)} collective-permute-done((bf16[2,9,128,128]{3,2,1,0:T(8,128)(2,1)}, bf16[2,9,128,128]{3,2,1,0:T(8,128)(2,1)S(1)}, u32[]{:S(2)}, u32[]{:S(2)}) %collective-permute-start) | collective-permute-done | bytes 589856 | tf_op jit(solution)/shard_map/ppermute | solution.py:14
  20.2 0.0 collective-permute-done.1
  20.2 3.3 %pad_maximum_fusion = bf16[12,9,128,128]{3,2,1,0:T(8,128)(2,1)} fusion(bf16[2,9,128,128]{3,2,1,0:T(8,128)(2,1)S(1)} %collective-permute-done.1, bf16[8,9,128,128]{3,2,1,0:T(8,128)(2,1)} %param.11, bf16[2,9,128,128]{3,2,1,0:T(8,128)(2,1)S(1)} %collective-permute-done), kind=kLoop, calls=%fused_computation.5 | loop fusion | flops 3538944 | bytes 7077888 | tf_op jit(solution)/shard_map/concatenate | solution.py:16
  23.5 11.4 %gather_fusion = bf16[192,128,128]{2,1,0:T(8,128)(2,1)} fusion(bf16[12,9,128,128]{3,2,1,0:T(8,128)(2,1)} %pad_maximum_fusion, s32[192]{0:T(256)S(1)} %reshape.136), kind=kCustom, calls=%fused_computation | custom fusion | bytes 12584448 | tf_op jit(solution)/shard_map/gather | solution.py:39
  35.0 7.3 %fusion.4 = bf16[12,4,128,256,1]{3,2,4,1,0:T(8,128)(2,1)} fusion(bf16[12,4,4,128,128]{4,3,2,1,0:T(8,128)(2,1)} %bitcast.36, bf16[12,4,128,256]{3,2,1,0:T(8,128)(2,1)} %param.12, bf16[12,4]{1,0:T(8,128)(2,1)S(1)} %get-tuple-element.37), kind=kOutput, calls=%fused_computation.9 | convolution fusion | flops 1612185600 | bytes 12583008 | tf_op jit(solution)/shard_map/bkjxy,bjyg->bkxg/dot_general | solution.py:40
  42.2 0.0 copy-done
  42.2 10.0 %convolution_bitcast_fusion = f32[12,4,4,128,128]{3,4,1,2,0:T(8,128)} fusion(f32[12,4]{1,0:T(8,128)S(1)} %get-tuple-element.38, f32[12,256]{1,0:T(8,128)S(1)} %copy-done.2, bf16[12,4,128,256]{3,2,1,0:T(8,128)(2,1)} %param.12, bf16[12,4,128,256,1]{3,2,4,1,0:T(8,128)(2,1)} %fusion.4, bf16[12,256,256]{2,1,0:T(8,128)(2,1)S(1)} %copy-done, ...), kind=kOutput, calls=%fused_computation.4 | convolution fusion | flops 2426929152 | bytes 20459808 | tf_op jit(solution)/shard_map/bkxg,bjyg->bkjxy/dot_general | solution.py:47
  52.2 12.6 %copy.16 = f32[12,4,4,128,128]{4,3,2,1,0:T(8,128)} copy(f32[12,4,4,128,128]{3,4,1,2,0:T(8,128)} %convolution_bitcast_fusion) | data formatting | bytes 25165824 | tf_op jit(solution)/shard_map/bkxg,bjyg->bkjxy/transpose | solution.py:47
  64.8 3.7 %broadcast_in_dim.4 = f32[12,9,128,128]{3,2,1,0:T(8,128)} broadcast(f32[]{:T(128)} %constant.66.clone.1), dimensions={} | broadcast | bytes 7077892 | tf_op jit(solution)/shard_map/broadcast_in_dim | solution.py:48
  68.5 41.0 %scatter_fusion = f32[12,9,128,128]{3,2,1,0:T(8,128)} fusion(f32[12,9,128,128]{3,2,1,0:T(8,128)} %broadcast_in_dim.4, s32[192]{0:T(256)S(1)} %reshape.142, f32[192,128,128]{2,1,0:T(8,128)} %bitcast.35), kind=kCustom, calls=%fused_computation.1 | custom fusion | flops 3145728 | bytes 37750272 | tf_op jit(solution)/shard_map/scatter-add | solution.py:49
  109.6 1.9 %fusion.21 = (f32[2,9,128,128]{3,2,1,0:T(8,128)S(1)}, f32[2,9,128,128]{3,2,1,0:T(8,128)S(1)}) fusion(f32[12,9,128,128]{3,2,1,0:T(8,128)} %scatter_fusion), kind=kLoop, calls=%fused_computation.37 | loop fusion | bytes 4718592 | tf_op jit(solution)/shard_map/slice | solution.py:52
  111.4 4.2 %collective-permute-start.2 = (f32[2,9,128,128]{3,2,1,0:T(8,128)S(1)}, f32[2,9,128,128]{3,2,1,0:T(8,128)S(1)}, u32[]{:S(2)}, u32[]{:S(2)}) collective-permute-start(f32[2,9,128,128]{3,2,1,0:T(8,128)S(1)} %get-tuple-element.32), channel_id=1, source_target_pairs={{0,1},{1,2},{2,3},{3,4},{4,5},{5,6},{6,7},{7,8},{8,9},{9,10},{10,1... | collective-permute-start | bytes 3538952 | tf_op jit(solution)/shard_map/ppermute | solution.py:23
  115.6 1.9 %collective-permute-start.3 = (f32[2,9,128,128]{3,2,1,0:T(8,128)S(1)}, f32[2,9,128,128]{3,2,1,0:T(8,128)S(1)}, u32[]{:S(2)}, u32[]{:S(2)}) collective-permute-start(f32[2,9,128,128]{3,2,1,0:T(8,128)S(1)} %get-tuple-element.31), channel_id=1, source_target_pairs={{1,0},{2,1},{3,2},{4,3},{5,4},{6,5},{7,6},{8,7},{9,8},{10,9},{11,1... | collective-permute-start | bytes 3538952 | tf_op jit(solution)/shard_map/ppermute | solution.py:23
  117.5 2.9 %slice.85 = f32[8,9,128,128]{3,2,1,0:T(8,128)S(1)} slice(f32[12,9,128,128]{3,2,1,0:T(8,128)} %scatter_fusion), slice={[2:10], [0:9], [0:128], [0:128]} | slice | bytes 9437184 | tf_op jit(solution)/shard_map/slice | solution.py:50
  120.4 20.9 %collective-permute-done.2 = f32[2,9,128,128]{3,2,1,0:T(8,128)S(1)} collective-permute-done((f32[2,9,128,128]{3,2,1,0:T(8,128)S(1)}, f32[2,9,128,128]{3,2,1,0:T(8,128)S(1)}, u32[]{:S(2)}, u32[]{:S(2)}) %collective-permute-start.2) | collective-permute-done | bytes 1179680 | tf_op jit(solution)/shard_map/ppermute | solution.py:23
  141.4 1.4 fusion.15
  142.8 0.0 copy-start.1
  142.8 0.0 collective-permute-done.3
  142.8 2.2 %copy-done.1 = f32[8,9,128,128]{3,2,1,0:T(8,128)} copy-done((f32[8,9,128,128]{3,2,1,0:T(8,128)}, f32[8,9,128,128]{3,2,1,0:T(8,128)S(1)}, u32[]{:S(2)}) %copy-start.1) | copy-done | bytes 4718616
  145.0 2.4 %fusion.14 = f32[8,9,128,128]{3,2,1,0:T(8,128)} fusion(f32[8,9,128,128]{3,2,1,0:T(8,128)} %copy-done.1, f32[2,9,128,128]{3,2,1,0:T(8,128)S(1)} %collective-permute-done.3), kind=kLoop, calls=%fused_computation.19 | loop fusion | flops 294912 | bytes 3538944 | tf_op jit(solution)/shard_map/scatter-add | solution.py:57
  (3 shorter events, 0.0 us)
Async XLA Ops:
  0.0 42.2 %copy-start = (bf16[12,256,256]{2,1,0:T(8,128)(2,1)S(1)}, bf16[12,256,256]{2,1,0:T(8,128)(2,1)}, u32[]{:S(2)}) copy-start(bf16[12,256,256]{2,1,0:T(8,128)(2,1)} %param.13) | copy-start | bytes 4718596
  2.3 18.0 %collective-permute-start = (bf16[2,9,128,128]{3,2,1,0:T(8,128)(2,1)}, bf16[2,9,128,128]{3,2,1,0:T(8,128)(2,1)S(1)}, u32[]{:S(2)}, u32[]{:S(2)}) collective-permute-start(bf16[2,9,128,128]{3,2,1,0:T(8,128)(2,1)} %get-tuple-element.33), channel_id=1, source_target_pairs={{0,1},{1,2},{2,3},{3,4},{4,5},{5,6},{6,7},{7,8},{8,9},{9,10},{10,1... | collective-permute-start | bytes 1769480 | tf_op jit(solution)/shard_map/ppermute | solution.py:14
  6.8 13.4 %collective-permute-start.1 = (bf16[2,9,128,128]{3,2,1,0:T(8,128)(2,1)S(1)}, bf16[2,9,128,128]{3,2,1,0:T(8,128)(2,1)S(1)}, u32[]{:S(2)}, u32[]{:S(2)}) collective-permute-start(bf16[2,9,128,128]{3,2,1,0:T(8,128)(2,1)S(1)} %get-tuple-element.34), channel_id=1, source_target_pairs={{1,0},{2,1},{3,2},{4,3},{5,4},{6,5},{7,6},{8,7},{9,8},{10,9},{11,1... | collective-permute-start | bytes 1769480 | tf_op jit(solution)/shard_map/ppermute | solution.py:15
  35.0 7.3 %copy-start.2 = (f32[12,256]{1,0:T(8,128)S(1)}, f32[12,256]{1,0:T(8,128)}, u32[]{:S(2)}) copy-start(f32[12,256]{1,0:T(8,128)} %param.14) | copy-start | bytes 36868
  111.4 29.9 %collective-permute-start.2 = (f32[2,9,128,128]{3,2,1,0:T(8,128)S(1)}, f32[2,9,128,128]{3,2,1,0:T(8,128)S(1)}, u32[]{:S(2)}, u32[]{:S(2)}) collective-permute-start(f32[2,9,128,128]{3,2,1,0:T(8,128)S(1)} %get-tuple-element.32), channel_id=1, source_target_pairs={{0,1},{1,2},{2,3},{3,4},{4,5},{5,6},{6,7},{7,8},{8,9},{9,10},{10,1... | collective-permute-start | bytes 3538952 | tf_op jit(solution)/shard_map/ppermute | solution.py:23
  115.6 27.2 %collective-permute-start.3 = (f32[2,9,128,128]{3,2,1,0:T(8,128)S(1)}, f32[2,9,128,128]{3,2,1,0:T(8,128)S(1)}, u32[]{:S(2)}, u32[]{:S(2)}) collective-permute-start(f32[2,9,128,128]{3,2,1,0:T(8,128)S(1)} %get-tuple-element.31), channel_id=1, source_target_pairs={{1,0},{2,1},{3,2},{4,3},{5,4},{6,5},{7,6},{8,7},{9,8},{10,9},{11,1... | collective-permute-start | bytes 3538952 | tf_op jit(solution)/shard_map/ppermute | solution.py:23
  142.8 2.2 %copy-start.1 = (f32[8,9,128,128]{3,2,1,0:T(8,128)}, f32[8,9,128,128]{3,2,1,0:T(8,128)S(1)}, u32[]{:S(2)}) copy-start(f32[8,9,128,128]{3,2,1,0:T(8,128)S(1)} %fusion.15) | copy-start | bytes 14155780
where the time goes:
time: 148 us; the launch traced here: 147 us
  other arithmetic  49.7 us (34%)
  local copies, waits for them, and re-layouts  37.5 us (25%)
  waiting for transfers between devices  30.4 us (21%)
  matrix products  17.2 us (12%)
  starting transfers between devices  12.5 us (8%)
    scatter-add x1, other arithmetic, local(): accumulated = accumulated.at[local_rows[:, :, None], bands].add(part)  41 us
    ppermute x2, waiting for transfers between devices, passed_along(): return lax.ppermute(shard, axis, pairs)  20.9 us
    transpose x1, local copies, waits for them, and re-layouts, local(): jnp.einsum('bkxg,bjyg->bkjxy', panel, hpanel, preferred_element_type=jnp....  12.6 us
    gather x1, local copies, waits for them, and re-layouts, local(): tiles = extended[local_rows[:, :, None], bands]  11.4 us
    dot_general x1, matrix products, local(): jnp.einsum('bkxg,bjyg->bkjxy', panel, hpanel, preferred_element_type=jnp....  9.97 us
    ppermute x1, waiting for transfers between devices, with_halo(): before = lax.ppermute(last, axis, up)  9.44 us
    dot_general x1, matrix products, local(): jnp.einsum('bkjxy,bjyg->bkxg', tiles, panel, preferred_element_type=jnp.f...  7.26 us
    ppermute x2, starting transfers between devices, passed_along(): return lax.ppermute(shard, axis, pairs)  6.09 us
  transfers between devices with their start and end apart: 4, of which 2 were waited for; matrix products, arithmetic and copies ran while one was open for 4% of the time, Pallas kernels for 0%

commit v1 on v0

v1 whole, which is shorter than its diff:
```python
import functools

import jax
import jax.numpy as jnp
from jax import lax
from jax.experimental import pallas as pl
from jax.experimental.pallas import tpu as pltpu
from jax.sharding import PartitionSpec as P

MIB = 1 << 20
GROUP = 2
LISTS = 6
SMEM_SPEC = pl.BlockSpec(memory_space=pltpu.SMEM)
VMEM_SPEC = pl.BlockSpec(memory_space=pltpu.VMEM)
ANY_SPEC = pl.BlockSpec(memory_space=pl.ANY)


class Geometry:
    def __init__(self, rows, band, batches, slots):
        self.rows, self.band, self.batches, self.slots = rows, band, batches, slots
        self.half = half = (band - 1) // 2
        self.reach = reach = half // 2
        self.own = rows * band
        low = [(-m, reach + m, band) for m in range(reach, 0, -1)]
        high = [(rows + m, 0, 3 * reach - m) for m in range(reach)]
        self.halo = sum(stop - start for _, start, stop in low)
        low_cut = [half - row for row, _, _ in low]
        high_cut = [rows - row + half for row, _, _ in high]
        early = (
            [(row, cut, stop) for (row, _, stop), cut in zip(low, low_cut)],
            [(row, start, cut) for (row, start, _), cut in zip(high, high_cut)],
        )
        late = (
            [(row, start, cut) for (row, start, _), cut in zip(low, low_cut)],
            [(row, cut, stop) for (row, _, stop), cut in zip(high, high_cut)],
        )
        self.early = sum(stop - start for _, start, stop in early[0])
        self.late = self.halo - self.early
        self.first_at = self.own
        self.early_at = self.own + self.halo
        self.late_at = self.early_at + self.early
        self.spare = self.late_at + self.late
        cut = (self.halo + 1) // 2
        self.pieces = ((0, cut), (cut, self.halo - cut))
        self.halo_base = self.bases((low, high))
        self.early_base = self.bases(early)
        self.late_base = self.bases(late)
        shifts = (rows, -rows)
        self.packs = [self.places(*pair) for pair in zip((low, high), shifts)]
        self.early_packs = [self.places(*pair) for pair in zip(early, shifts)]
        self.late_packs = [self.places(*pair) for pair in zip(late, shifts)]
        touched = set()
        for start, _, count in self.packs[0] + self.packs[1]:
            touched.update(range(start, start + count))
        self.quiet = []
        for index in range(self.own):
            if index in touched:
                continue
            if self.quiet and sum(self.quiet[-1]) == index:
                self.quiet[-1] = (self.quiet[-1][0], self.quiet[-1][1] + 1)
            else:
                self.quiet.append((index, 1))
        self.list_size = batches + 2
        self.lengths_at = LISTS * self.list_size
        self.local_at = self.lengths_at + LISTS
        self.count_at = self.local_at + batches
        self.offsets_at = self.count_at + batches
        self.meta_size = self.offsets_at + slots * batches

    def bases(self, sides):
        found = {}
        for segments in sides:
            place = 0
            for row, start, stop in segments:
                found[row] = place - start
                place += stop - start
        return found

    def places(self, segments, shift):
        pack, place = ([], 0)
        for row, start, stop in segments:
            pack.append(((row + shift) * self.band + start, place, stop - start))
            place += stop - start
        return pack

    def near_packs(self, piece):
        begin, count = self.pieces[piece]
        found = []
        for pack in self.packs:
            part = []
            for start, place, size in pack:
                low, high = max(place, begin), min(place + size, begin + count)
                if low < high:
                    part.append((start + low - place, low - begin, high - low))
            found.append(part)
        return found

    def pick(self, bases, shift, row, otherwise):
        value = otherwise
        for at, base in bases.items():
            value = jnp.where(row == at, base + shift, value)
        return value


def run_copies(copies):
    for copy in copies:
        copy.start()
    for copy in copies:
        copy.wait()


def by_parity(index_ref, body, first, second):
    odd = index_ref[0] % 2 == 1

    @pl.when(jnp.logical_not(odd))
    def _():
        body(first, second)

    @pl.when(odd)
    def _():
        body(second, first)


def pack_copies(geo, index_ref, density_ref, out_ref, sems, first, act):
    odd = index_ref[0] % 2 == 1
    upper = jnp.logical_not(odd) if first else odd
    for pack, chosen in zip(geo.packs, (upper, jnp.logical_not(upper))):

        @pl.when(chosen)
        def _(pack=pack):
            for i, (start, place, count) in enumerate(pack):
                act(
                    pltpu.make_async_copy(
                        density_ref.at[pl.ds(start, count)], out_ref.at[pl.ds(place, count)], sems.at[i]
                    )
                )


def pack_kernel(geo, index_ref, density_ref, first_ref, second_ref, sems):
    packing = (geo, index_ref, density_ref)
    for act in (lambda copy: copy.start(), lambda copy: copy.wait()):
        pack_copies(*packing, second_ref, sems.at[1], False, act)
        pack_copies(*packing, first_ref, sems.at[0], True, act)


CROSS_MANY, CROSS_FEW, NEAR_MANY, NEAR_FEW, INNER_MANY, INNER_FEW = range(LISTS)


def build_lists(geo, index_ref, centre_ref, offsets_ref, counts_ref, meta_ref):
    first = index_ref[0] * geo.rows
    odd = index_ref[0] % 2 == 1
    lengths = [jnp.int32(0)] * LISTS
    for b in range(geo.batches):
        local = centre_ref[b] - first
        count = counts_ref[b]
        meta_ref[geo.local_at + b] = local
        meta_ref[geo.count_at + b] = count
        low = high = jnp.bool_(False)
        for k in range(geo.slots):
            offset = offsets_ref[k, b]
            meta_ref[geo.offsets_at + k * geo.batches + b] = offset
            row = local + offset
            low = low | ((k < count) & (row < 0))
            high = high | ((k < count) & (row >= geo.rows))
        cross = (odd & high) | (jnp.logical_not(odd) & low)
        near = (odd & low) | (jnp.logical_not(odd) & high)
        inner = jnp.logical_not(low | high)
        many = count > 2
        few = (count > 0) & jnp.logical_not(many)
        kinds = [kind & size for kind in (cross, near, inner) for size in (many, few)]
        for which, member in enumerate(kinds):
            meta_ref[which * geo.list_size + lengths[which]] = b
            lengths[which] = lengths[which] + member.astype(jnp.int32)
    for which in range(LISTS):
        meta_ref[which * geo.list_size + lengths[which]] = geo.batches
        meta_ref[geo.lengths_at + which] = lengths[which]


def each_group(geo, meta_ref, which, size, body):
    length = meta_ref[geo.lengths_at + which]

    def step(i, carry):
        chosen = []
        for n in range(size):
            place = i * size + n
            there = place < length
            b = meta_ref[which * geo.list_size + jnp.minimum(place, length)]
            chosen.append((jnp.where(there, b, 0), there))
        body(chosen)
        return carry

    lax.fori_loop(0, (length + size - 1) // size, step, 0)


class Slots:
    def __init__(self, geo, meta_ref, b, there, width):
        local = meta_ref[geo.local_at + b]
        count = jnp.where(there, meta_ref[geo.count_at + b], 0)
        self.offset = [meta_ref[geo.offsets_at + k * geo.batches + b] for k in range(width)]
        self.local = local
        self.row = [local + offset for offset in self.offset]
        self.live = [k < count for k in range(width)]
        self.own = [(row >= 0) & (row < geo.rows) for row in self.row]
        self.width = width


def panels(slots, ao_ref, b):
    return jnp.concatenate(
        [
            ao_ref[b, k] * jnp.where(slots.live[k], 1.0, 0.0).astype(ao_ref.dtype)
            for k in range(slots.width)
        ],
        axis=0,
    )


def gathered(tiles_ref, places):
    return jnp.concatenate(
        [jnp.concatenate([tiles_ref[place] for place in row], axis=1) for row in places], axis=0
    )


def chain(xs, tiles, batches, kernel_ref, weights_ref):
    fs = [
        jnp.dot(t, x, preferred_element_type=jnp.float32).astype(jnp.bfloat16)
        for t, x in zip(tiles, xs)
    ]
    gs = [
        jnp.dot(f, kernel_ref[b], preferred_element_type=jnp.float32) for f, b in zip(fs, batches)
    ]
    hs = [(g * weights_ref[pl.ds(b, 1), :]).astype(jnp.bfloat16) for g, b in zip(gs, batches)]
    return [
        lax.dot_general(x, h, (((1,), (1,)), ((), ())), preferred_element_type=jnp.float32)
        for x, h in zip(xs, hs)
    ]


def scatter(part, target, nb, acc_ref):
    for k, row in enumerate(target):
        for j, place in enumerate(row):
            acc_ref[place] += part[k * nb : (k + 1) * nb, j * nb : (j + 1) * nb]


def add_whole(geo, chosen, width, meta_ref, tiles_ref, ao_ref, kernel_ref, weights_ref, acc_ref):
    xs, tiles, targets = ([], [], [])
    for b, there in chosen:
        slots = Slots(geo, meta_ref, b, there, width)
        xs.append(panels(slots, ao_ref, b))
        places, target = ([], [])
        for k in range(width):
            row = slots.row[k]
            base = jnp.where(slots.live[k] & slots.own[k], row, 0) * geo.band
            base = jnp.where(
                slots.live[k], geo.pick(geo.halo_base, geo.first_at, row, base), base
            )
            place = [base + slots.offset[j] - slots.offset[k] + geo.half for j in range(width)]
            places.append(place)
            target.append(
                [jnp.where(slots.live[k] & slots.live[j], place[j], geo.spare) for j in range(width)]
            )
        tiles.append(gathered(tiles_ref, places))
        targets.append(target)
    parts = chain(xs, tiles, [b for b, _ in chosen], kernel_ref, weights_ref)
    for part, target in zip(parts, targets):
        scatter(part, target, ao_ref.shape[2], acc_ref)


def add_own(geo, chosen, width, meta_ref, tiles_ref, ao_ref, kernel_ref, weights_ref, acc_ref):
    xs, tiles, targets = ([], [], [])
    for b, there in chosen:
        slots = Slots(geo, meta_ref, b, there, width)
        xs.append(panels(slots, ao_ref, b))
        places, target = ([], [])
        for k in range(width):
            row = slots.row[k]
            band = [slots.offset[j] - slots.offset[k] + geo.half for j in range(width)]
            base = jnp.where(slots.own[k], row, 0) * geo.band
            places.append([base + o for o in band])
            base = geo.pick(geo.early_base, geo.early_at, row, base)
            target.append(
                [
                    jnp.where(
                        slots.live[k] & slots.live[j] & slots.own[j], base + band[j], geo.spare
                    )
                    for j in range(width)
                ]
            )
        tiles.append(gathered(tiles_ref, places))
        targets.append(target)
    parts = chain(xs, tiles, [b for b, _ in chosen], kernel_ref, weights_ref)
    for part, target in zip(parts, targets):
        scatter(part, target, ao_ref.shape[2], acc_ref)


def add_halo(geo, chosen, width, meta_ref, halo_ref, ao_ref, kernel_ref, weights_ref, acc_ref):
    outer = min(geo.reach, width)
    xs, tiles, targets = ([], [], [])
    for b, there in chosen:
        slots = Slots(geo, meta_ref, b, there, width)
        xs.append(panels(slots, ao_ref, b))
        found = jnp.int32(0)
        picked = [jnp.int32(0)] * outer
        for k in range(width):
            away = slots.live[k] & jnp.logical_not(slots.own[k])
            for i in range(outer):
                picked[i] = jnp.where(away & (found <= i), slots.offset[k], picked[i])
            found = found + away.astype(jnp.int32)
        places, target = ([], [[None] * outer for _ in range(width)])
        for i in range(outer):
            base = geo.pick(geo.halo_base, 0, slots.local + picked[i], 0)
            places.append(
                [
                    jnp.where(there, base + slots.offset[j] - picked[i] + geo.half, 0)
                    for j in range(width)
                ]
            )
        for k in range(width):
            row = slots.row[k]
            base = geo.pick(geo.late_base, geo.late_at, row, row * geo.band)
            for i in range(outer):
                target[k][i] = jnp.where(
                    slots.live[k] & (i < found),
                    base + picked[i] - slots.offset[k] + geo.half,
                    geo.spare,
                )
        tiles.append(gathered(halo_ref, places))
        targets.append(target)
    parts = chain(xs, tiles, [b for b, _ in chosen], kernel_ref, weights_ref)
    for part, target in zip(parts, targets):
        scatter(part, target, ao_ref.shape[2], acc_ref)


def early_kernel(
    geo, index_ref, centre_ref, offsets_ref, counts_ref, density_ref, ao_ref, kernel_ref, weights_ref,
    meta_ref, tiles_ref, acc_ref, early_out, sem,
):
    copy = pltpu.make_async_copy(density_ref, tiles_ref.at[pl.ds(0, geo.own)], sem)
    copy.start()
    build_lists(geo, index_ref, centre_ref, offsets_ref, counts_ref, meta_ref)
    acc_ref[...] = jnp.zeros_like(acc_ref)
    copy.wait()
    refs = (meta_ref, tiles_ref, ao_ref, kernel_ref, weights_ref, acc_ref)
    for which, width in ((CROSS_MANY, geo.slots), (CROSS_FEW, 2)):
        each_group(
            geo, meta_ref, which, GROUP, lambda chosen, width=width: add_own(geo, chosen, width, *refs)
        )
    early_out[...] = acc_ref[pl.ds(geo.early_at, geo.early)].astype(early_out.dtype)


def near_kernel(
    geo, meta_ref, halo_ref, ao_ref, kernel_ref, weights_ref, tiles_in, acc_in,
    tiles_ref, acc_ref, *rest,
):
    outs, sem = rest[:-1], rest[-1]
    run_copies(
        [pltpu.make_async_copy(halo_ref, tiles_ref.at[pl.ds(geo.first_at, geo.halo)], sem)]
    )
    refs = (meta_ref, tiles_ref, ao_ref, kernel_ref, weights_ref, acc_ref)
    for which, width in ((NEAR_MANY, geo.slots), (NEAR_FEW, 2)):
        each_group(
            geo, meta_ref, which, GROUP, lambda chosen, width=width: add_whole(geo, chosen, width, *refs)
        )
    for out, (start, count) in zip(outs, geo.pieces):
        out[...] = acc_ref[pl.ds(geo.first_at + start, count)].astype(out.dtype)


def late_kernel(
    geo, meta_ref, halo_ref, ao_ref, kernel_ref, weights_ref, acc_in, acc_ref, late_out
):
    refs = (meta_ref, halo_ref, ao_ref, kernel_ref, weights_ref, acc_ref)
    for which, width in ((CROSS_MANY, geo.slots), (CROSS_FEW, 2)):
        each_group(
            geo, meta_ref, which, GROUP, lambda chosen, width=width: add_halo(geo, chosen, width, *refs)
        )
    late_out[...] = acc_ref[pl.ds(geo.late_at, geo.late)].astype(late_out.dtype)


def inner_kernel(
    geo, meta_ref, tiles_ref, ao_ref, kernel_ref, weights_ref, acc_in, acc_ref, out_ref, sems
):
    refs = (meta_ref, tiles_ref, ao_ref, kernel_ref, weights_ref, acc_ref)
    for which, width in ((INNER_MANY, geo.slots), (INNER_FEW, 2)):
        each_group(
            geo, meta_ref, which, GROUP, lambda chosen, width=width: add_whole(geo, chosen, width, *refs)
        )
    run_copies(
        [
            pltpu.make_async_copy(
                acc_ref.at[pl.ds(start, count)], out_ref.at[pl.ds(start, count)], sems.at[i]
            )
            for i, (start, count) in enumerate(geo.quiet)
        ]
    )


def finish_kernel(
    geo, index_ref, early_ref, late_ref, near_a, near_b, acc_ref, out_in, out_ref, total, sems
):
    def add(up, down):
        copies = []
        for side, parts in enumerate((up, down)):
            for packs, ref in parts:
                for start, place, count in packs[side]:
                    spot = pl.ds(len(copies) * geo.band, count)
                    total[spot] = acc_ref[pl.ds(start, count)] + ref[pl.ds(place, count)].astype(
                        jnp.float32
                    )
                    copy = pltpu.make_async_copy(
                        total.at[spot], out_ref.at[pl.ds(start, count)], sems.at[len(copies)]
                    )
                    copy.start()
                    copies.append(copy)
        for copy in copies:
            copy.wait()

    near = ((geo.near_packs(0), near_a), (geo.near_packs(1), near_b))
    by_parity(index_ref, add, near, ((geo.early_packs, early_ref), (geo.late_packs, late_ref)))


def call(kernel, out_shape, in_specs, out_specs, scratch, aliases=None, cost=None):
    return pl.pallas_call(
        kernel,
        out_shape=out_shape,
        in_specs=in_specs,
        out_specs=out_specs,
        scratch_shapes=scratch,
        input_output_aliases=aliases or {},
        cost_estimate=cost,
        compiler_params=pltpu.CompilerParams(vmem_limit_bytes=16 * MIB),
    )


def to_first(x, size):
    pairs = [(i, i + 1) for i in range(0, size - 1, 2)]
    got = lax.ppermute(x, "blk", pairs + [(j, i) for i, j in pairs])
    return pltpu.with_memory_space_constraint(got, pltpu.VMEM)


def to_second(x, size):
    pairs = [(i, i + 1) for i in range(1, size - 1, 2)]
    got = lax.ppermute(x, "blk", pairs + [(j, i) for i, j in pairs])
    return pltpu.with_memory_space_constraint(got, pltpu.VMEM)


def local(density, ao_values, kernel, grid_weights, centre, sig_offsets, counts):
    rows, band, nb, _ = density.shape
    batches, slots, _, pts = ao_values.shape
    size = lax.axis_size("blk")
    geo = Geometry(rows, band, batches, slots)
    index = lax.axis_index("blk").astype(jnp.int32).reshape(1)
    in_hbm = lambda x: pltpu.with_memory_space_constraint(x, pltpu.HBM)
    flat = in_hbm(density.reshape(geo.own, nb, nb))
    pack = lambda count: pltpu.VMEM((count, nb, nb), jnp.bfloat16)
    dma = pltpu.SemaphoreType.DMA
    tiles_type = pltpu.VMEM((geo.own + geo.halo, nb, nb), jnp.bfloat16)
    acc_type = pltpu.VMEM((geo.spare + 1, nb, nb), jnp.float32)

    near_halo, cross_halo = call(
        functools.partial(pack_kernel, geo),
        (pack(geo.halo),) * 2,
        [SMEM_SPEC, ANY_SPEC],
        (VMEM_SPEC,) * 2,
        [dma((2, geo.reach))],
        cost=pl.CostEstimate(flops=10**10, bytes_accessed=10**8, transcendentals=0),
    )(index, flat)
    cross_halo = to_second(cross_halo, size)
    near_halo = to_first(near_halo, size)

    panel = (ao_values, kernel, grid_weights)
    meta, tiles, acc, early = call(
        functools.partial(early_kernel, geo),
        (pltpu.SMEM((geo.meta_size,), jnp.int32), tiles_type, acc_type, pack(geo.early)),
        [SMEM_SPEC] * 4 + [ANY_SPEC] + [VMEM_SPEC] * 3,
        (SMEM_SPEC,) + (VMEM_SPEC,) * 3,
        [dma],
    )(index, in_hbm(centre), in_hbm(sig_offsets.T), in_hbm(counts), flat, *panel)
    early = to_second(early, size)

    tiles, acc, *near = call(
        functools.partial(near_kernel, geo),
        (tiles_type, acc_type) + tuple(pack(count) for _, count in geo.pieces),
        [SMEM_SPEC] + [VMEM_SPEC] * 6,
        (VMEM_SPEC,) * 4,
        [dma],
        {5: 0, 6: 1},
    )(meta, near_halo, *panel, tiles, acc)
    near = [to_first(piece, size) for piece in near]

    acc, late = call(
        functools.partial(late_kernel, geo),
        (acc_type, pack(geo.late)),
        [SMEM_SPEC] + [VMEM_SPEC] * 5,
        (VMEM_SPEC,) * 2,
        [],
        {5: 0},
    )(meta, cross_halo, *panel, acc)
    late = to_second(late, size)

    whole = jax.ShapeDtypeStruct((geo.own, nb, nb), jnp.float32)
    acc, out = call(
        functools.partial(inner_kernel, geo),
        (acc_type, whole),
        [SMEM_SPEC] + [VMEM_SPEC] * 5,
        (VMEM_SPEC, ANY_SPEC),
        [dma((len(geo.quiet),))],
        {5: 0},
    )(meta, tiles, *panel, acc)

    pieces = 2 * (2 * geo.reach)
    out = call(
        functools.partial(finish_kernel, geo),
        whole,
        [SMEM_SPEC] + [VMEM_SPEC] * 5 + [ANY_SPEC],
        ANY_SPEC,
        [pltpu.VMEM((pieces * band, nb, nb), jnp.float32), dma((pieces,))],
        {6: 0},
    )(index, early, late, *near, acc, out)
    return out.reshape(rows, band, nb, nb)


def solution(mesh):
    placed = (
        P(("groups", "blk"), None, None, None),
        P(("groups", "blk"), None, None, None),
        P(("groups", "blk"), None, None),
        P(("groups", "blk"), None),
        P(("groups", "blk")),
        P(("groups", "blk"), None),
        P(("groups", "blk")),
    )
    return jax.shard_map(
        local,
        mesh=mesh,
        in_specs=placed,
        out_specs=P(("groups", "blk"), None, None, None),
        check_vma=False,
    )
```

time: 148 us -> 27.9 us (0.19)
  the two profiles are of different devices: /device:TPU:1 before, /device:TPU:25 now
where the time goes in v1:
time: 27.9 us; the launch traced here: 27.6 us
  Pallas kernels  14.5 us (52%)
  starting transfers between devices  9.41 us (34%)
  waiting for transfers between devices  3.6 us (13%)
    ppermute x3, starting transfers between devices, to_second(): got = lax.ppermute(x, 'blk', pairs + [(j, i) for i, j in pairs])  7.47 us
    pallas_call x1, Pallas kernels, local(): call(functools.partial(inner_kernel, geo), (acc_type, whole), [SMEM_SPEC]...  6.37 us
    ppermute x3, waiting for transfers between devices, to_second(): got = lax.ppermute(x, 'blk', pairs + [(j, i) for i, j in pairs])  3.59 us
    pallas_call x1, Pallas kernels, local(): call(functools.partial(early_kernel, geo), (pltpu.SMEM((geo.meta_size,),...  3.42 us
    ppermute x3, starting transfers between devices, to_first(): got = lax.ppermute(x, 'blk', pairs + [(j, i) for i, j in pairs])  1.94 us
    pallas_call x1, Pallas kernels, local(): call(functools.partial(pack_kernel, geo), (pack(geo.halo),) * 2, [SMEM_SP...  1.38 us
    pallas_call x1, Pallas kernels, local(): call(functools.partial(near_kernel, geo), (tiles_type, acc_type) + tuple(...  1.23 us
    pallas_call x1, Pallas kernels, local(): call(functools.partial(finish_kernel, geo), whole, [SMEM_SPEC] + [VMEM_SP...  1.19 us
  transfers between devices with their start and end apart: 6, of which 1 were waited for; matrix products, arithmetic and copies ran while one was open for 0% of the time, Pallas kernels for 43%

profile of v1, /device:TPU:25, one launch (start us, length us, event | category | flops | bytes accessed | tf_op | source)
XLA Modules:
  0.0 27.6 jit_solution(11668421749355326060)
XLA Ops:
  0.0 0.0 copy-start
  0.0 0.0 copy-start.1
  0.0 0.0 copy-start.2
  0.0 1.4 %shard_map.74 = (bf16[11,128,128]{2,1,0:T(8,128)(2,1)S(1)}, bf16[11,128,128]{2,1,0:T(8,128)(2,1)S(1)}) custom-call(s32[1]{0:T(128)} %bitcast.index_ref, bf16[72,128,128]{2,1,0:T(8,128)(2,1)} %bitcast.4), custom_call_target="tpu_custom_call" | custom-call | flops 10000000000 | bytes 100000000 | tf_op jit(solution)/shard_map/pallas_call | solution.py:458
  1.4 0.7 %collective-permute-start.2 = (bf16[11,128,128]{2,1,0:T(8,128)(2,1)S(1)}, bf16[11,128,128]{2,1,0:T(8,128)(2,1)S(1)}, u32[]{:S(2)}, u32[]{:S(2)}) collective-permute-start(bf16[11,128,128]{2,1,0:T(8,128)(2,1)S(1)} %get-tuple-element.22), channel_id=1, source_target_pairs={{0,1},{2,3},{4,5},{6,7},{8,9},{10,11},{12,13},{14,15},{1,0},{3,2},... | collective-permute-start | bytes 1081352 | tf_op jit(solution)/shard_map/ppermute | solution.py:435
  2.1 3.2 %collective-permute-start.1 = (bf16[11,128,128]{2,1,0:T(8,128)(2,1)S(1)}, bf16[11,128,128]{2,1,0:T(8,128)(2,1)S(1)}, u32[]{:S(2)}, u32[]{:S(2)}) collective-permute-start(bf16[11,128,128]{2,1,0:T(8,128)(2,1)S(1)} %get-tuple-element.21), channel_id=1, source_target_pairs={{1,2},{3,4},{5,6},{7,8},{9,10},{11,12},{13,14},{2,1},{4,3},{6,5},{... | collective-permute-start | bytes 1081352 | tf_op jit(solution)/shard_map/ppermute | solution.py:441
  5.3 0.0 copy-done
  5.3 0.0 copy-done.1
  5.3 0.0 copy-done.2
  5.3 3.4 %shard_map.73 = (s32[162]{0:T(256)S(4)}, bf16[83,128,128]{2,1,0:T(8,128)(2,1)S(1)}, f32[95,128,128]{2,1,0:T(8,128)S(1)}, bf16[7,128,128]{2,1,0:T(8,128)(2,1)S(1)}) custom-call(s32[1]{0:T(128)} %bitcast.index_ref, s32[12]{0:T(128)} %centre_ref.1, s32[4,12]{1,0:T(4,128)} %bitcast.6, s32[12]{0:T(128)} %counts_ref.1, bf16[72,128,128]{2,1,0:T(8,128)(2,1)} %bitcast.5, ...), custom_call_target="tpu_custom_call" | custom-call | tf_op jit(solution)/shard_map/pallas_call | solution.py:470
  8.8 2.4 %collective-permute-start = (bf16[7,128,128]{2,1,0:T(8,128)(2,1)S(1)}, bf16[7,128,128]{2,1,0:T(8,128)(2,1)S(1)}, u32[]{:S(2)}, u32[]{:S(2)}) collective-permute-start(bf16[7,128,128]{2,1,0:T(8,128)(2,1)S(1)} %get-tuple-element.19), channel_id=1, source_target_pairs={{1,2},{3,4},{5,6},{7,8},{9,10},{11,12},{13,14},{2,1},{4,3},{6,5},{... | collective-permute-start | bytes 688136 | tf_op jit(solution)/shard_map/ppermute | solution.py:441
  11.2 0.0 collective-permute-done.2.halo_ref
  11.2 1.2 %shard_map.75 = (bf16[83,128,128]{2,1,0:T(8,128)(2,1)S(1)}, f32[95,128,128]{2,1,0:T(8,128)S(1)}, bf16[6,128,128]{2,1,0:T(8,128)(2,1)S(1)}, bf16[5,128,128]{2,1,0:T(8,128)(2,1)S(1)}) custom-call(s32[162]{0:T(256)S(4)} %get-tuple-element.20.meta_ref, ...), custom_call_target="tpu_custom_call", output_to_operand_aliasing={{0}: (5, {}), {1}: (6, {})} | custom-call | tf_op jit(solution)/shard_map/pallas_call | solution.py:479
  12.4 1.1 %collective-permute-start.4 = (bf16[6,128,128]{2,1,0:T(8,128)(2,1)S(1)}, bf16[6,128,128]{2,1,0:T(8,128)(2,1)S(1)}, u32[]{:S(2)}, u32[]{:S(2)}) collective-permute-start(bf16[6,128,128]{2,1,0:T(8,128)(2,1)S(1)} %get-tuple-element.27), channel_id=1, source_target_pairs={{0,1},{2,3},{4,5},{6,7},{8,9},{10,11},{12,13},{14,15},{1,0},{3,2},... | collective-permute-start | bytes 589832 | tf_op jit(solution)/shard_map/ppermute | solution.py:435
  13.5 0.1 collective-permute-start.5
  13.6 3.6 %collective-permute-done.1.halo_ref = bf16[11,128,128]{2,1,0:T(8,128)(2,1)S(1)} collective-permute-done((bf16[11,128,128]{2,1,0:T(8,128)(2,1)S(1)}, bf16[11,128,128]{2,1,0:T(8,128)(2,1)S(1)}, u32[]{:S(2)}, u32[]{:S(2)}) %collective-permute-start.1) | collective-permute-done | bytes 360480 | tf_op jit(solution)/shard_map/ppermute | solution.py:441
  17.2 0.9 %shard_map.76 = (f32[95,128,128]{2,1,0:T(8,128)S(1)}, bf16[4,128,128]{2,1,0:T(8,128)(2,1)S(1)}) custom-call(s32[162]{0:T(256)S(4)} %get-tuple-element.20.meta_ref, bf16[11,128,128]{2,1,0:T(8,128)(2,1)S(1)} %collective-permute-done.1.halo_ref, bf16[12,4,128,256]{3,2,1,0:T(8,128)(2,1)S(1)} %copy-done, ...), custom_call_target="tpu_custom_call", output_to_operand_aliasing={{0}: (5, {})} | custom-call | tf_op jit(solution)/shard_map/pallas_call | solution.py:489
  18.1 1.9 %collective-permute-start.3 = (bf16[4,128,128]{2,1,0:T(8,128)(2,1)S(1)}, bf16[4,128,128]{2,1,0:T(8,128)(2,1)S(1)}, u32[]{:S(2)}, u32[]{:S(2)}) collective-permute-start(bf16[4,128,128]{2,1,0:T(8,128)(2,1)S(1)} %get-tuple-element.26), channel_id=1, source_target_pairs={{1,2},{3,4},{5,6},{7,8},{9,10},{11,12},{13,14},{2,1},{4,3},{6,5},{... | collective-permute-start | bytes 393224 | tf_op jit(solution)/shard_map/ppermute | solution.py:441
  20.0 6.4 %shard_map.77 = (f32[95,128,128]{2,1,0:T(8,128)S(1)}, f32[72,128,128]{2,1,0:T(8,128)}) custom-call(s32[162]{0:T(256)S(4)} %get-tuple-element.20.meta_ref, bf16[83,128,128]{2,1,0:T(8,128)(2,1)S(1)} %get-tuple-element.29.tiles_ref, bf16[12,4,128,256]{3,2,1,0:T(8,128)(2,1)S(1)} %copy-done, ...), custom_call_target="tpu_custom_call", output_to_operand_aliasing={{0}: (5, {})} | custom-call | tf_op jit(solution)/shard_map/pallas_call | solution.py:500
  26.4 0.0 collective-permute-done.early_ref
  26.4 0.0 collective-permute-done.3.late_ref
  26.4 0.0 collective-permute-done.5.near_b
  26.4 0.0 collective-permute-done.4.near_a
  26.4 1.2 %shard_map.78 = f32[72,128,128]{2,1,0:T(8,128)} custom-call(s32[1]{0:T(128)} %bitcast.index_ref, bf16[7,128,128]{2,1,0:T(8,128)(2,1)S(1)} %collective-permute-done.early_ref, bf16[4,128,128]{2,1,0:T(8,128)(2,1)S(1)} %collective-permute-done.3.late_ref, bf16[6,128,128]{2,1,0:T(8,128)(2,1)S(1)} %collective-permute-done.4.near_a, ...), custom_call_target="tpu_custom_call", output_to_operand_aliasing={{}: (6, {})} | custom-call | tf_op jit(solution)/shard_map/pallas_call | solution.py:510
Async XLA Ops:
  0.0 5.3 %copy-start = (bf16[12,4,128,256]{3,2,1,0:T(8,128)(2,1)S(1)}, bf16[12,4,128,256]{3,2,1,0:T(8,128)(2,1)}, u32[]{:S(2)}) copy-start(bf16[12,4,128,256]{3,2,1,0:T(8,128)(2,1)} %ao_ref.7) | copy-start | bytes 9437188
  0.0 5.3 %copy-start.1 = (bf16[12,256,256]{2,1,0:T(8,128)(2,1)S(1)}, bf16[12,256,256]{2,1,0:T(8,128)(2,1)}, u32[]{:S(2)}) copy-start(bf16[12,256,256]{2,1,0:T(8,128)(2,1)} %kernel_ref.7) | copy-start | bytes 4718596
  0.0 5.3 %copy-start.2 = (f32[12,256]{1,0:T(8,128)S(1)}, f32[12,256]{1,0:T(8,128)}, u32[]{:S(2)}) copy-start(f32[12,256]{1,0:T(8,128)} %weights_ref.7) | copy-start | bytes 36868
  1.4 9.8 %collective-permute-start.2 = (bf16[11,128,128]{2,1,0:T(8,128)(2,1)S(1)}, bf16[11,128,128]{2,1,0:T(8,128)(2,1)S(1)}, u32[]{:S(2)}, u32[]{:S(2)}) collective-permute-start(bf16[11,128,128]{2,1,0:T(8,128)(2,1)S(1)} %get-tuple-element.22), channel_id=1, source_target_pairs={{0,1},{2,3},{4,5},{6,7},{8,9},{10,11},{12,13},{14,15},{1,0},{3,2},... | collective-permute-start | bytes 1081352 | tf_op jit(solution)/shard_map/ppermute | solution.py:435
  2.1 15.1 %collective-permute-start.1 = (bf16[11,128,128]{2,1,0:T(8,128)(2,1)S(1)}, bf16[11,128,128]{2,1,0:T(8,128)(2,1)S(1)}, u32[]{:S(2)}, u32[]{:S(2)}) collective-permute-start(bf16[11,128,128]{2,1,0:T(8,128)(2,1)S(1)} %get-tuple-element.21), channel_id=1, source_target_pairs={{1,2},{3,4},{5,6},{7,8},{9,10},{11,12},{13,14},{2,1},{4,3},{6,5},{... | collective-permute-start | bytes 1081352 | tf_op jit(solution)/shard_map/ppermute | solution.py:441
  8.8 17.6 %collective-permute-start = (bf16[7,128,128]{2,1,0:T(8,128)(2,1)S(1)}, bf16[7,128,128]{2,1,0:T(8,128)(2,1)S(1)}, u32[]{:S(2)}, u32[]{:S(2)}) collective-permute-start(bf16[7,128,128]{2,1,0:T(8,128)(2,1)S(1)} %get-tuple-element.19), channel_id=1, source_target_pairs={{1,2},{3,4},{5,6},{7,8},{9,10},{11,12},{13,14},{2,1},{4,3},{6,5},{... | collective-permute-start | bytes 688136 | tf_op jit(solution)/shard_map/ppermute | solution.py:441
  12.4 14.0 %collective-permute-start.4 = (bf16[6,128,128]{2,1,0:T(8,128)(2,1)S(1)}, bf16[6,128,128]{2,1,0:T(8,128)(2,1)S(1)}, u32[]{:S(2)}, u32[]{:S(2)}) collective-permute-start(bf16[6,128,128]{2,1,0:T(8,128)(2,1)S(1)} %get-tuple-element.27), channel_id=1, source_target_pairs={{0,1},{2,3},{4,5},{6,7},{8,9},{10,11},{12,13},{14,15},{1,0},{3,2},... | collective-permute-start | bytes 589832 | tf_op jit(solution)/shard_map/ppermute | solution.py:435
  13.5 12.9 %collective-permute-start.5 = (bf16[5,128,128]{2,1,0:T(8,128)(2,1)S(1)}, bf16[5,128,128]{2,1,0:T(8,128)(2,1)S(1)}, u32[]{:S(2)}, u32[]{:S(2)}) collective-permute-start(bf16[5,128,128]{2,1,0:T(8,128)(2,1)S(1)} %get-tuple-element.28), channel_id=1, source_target_pairs={{0,1},{2,3},{4,5},{6,7},{8,9},{10,11},{12,13},{14,15},{1,0},{3,2},... | collective-permute-start | bytes 491528 | tf_op jit(solution)/shard_map/ppermute | solution.py:435
  18.1 8.3 %collective-permute-start.3 = (bf16[4,128,128]{2,1,0:T(8,128)(2,1)S(1)}, bf16[4,128,128]{2,1,0:T(8,128)(2,1)S(1)}, u32[]{:S(2)}, u32[]{:S(2)}) collective-permute-start(bf16[4,128,128]{2,1,0:T(8,128)(2,1)S(1)} %get-tuple-element.26), channel_id=1, source_target_pairs={{1,2},{3,4},{5,6},{7,8},{9,10},{11,12},{13,14},{2,1},{4,3},{6,5},{... | collective-permute-start | bytes 393224 | tf_op jit(solution)/shard_map/ppermute | solution.py:441
